TPU v7x, 256 devices: a whole 4x4x8 slice. The times are simulated.
256 devices in a mesh: prompt: 16 (over y, x_hi, core), resp: 16 (over x_lo, z).
Axes of the slice: x: 4 (x_hi: 2, x_lo: 2; x = x_hi * 2 + x_lo), y: 4, z: 8, core: 2. Of those that a mesh axis runs over, the one named last changes fastest.
Arguments:
- q_prefix: bfloat16 [16, 1024, 1024], P('prompt', 'resp'), may hold values from -40 to 40
- q_resp: bfloat16 [16, 4, 1024, 1024], P('prompt', None, 'resp'), may hold values from -40 to 40
- k_prefix: bfloat16 [16, 1024, 128], P('prompt', 'resp'), may hold values from -6 to 6
- v_prefix: bfloat16 [16, 1024, 128], P('prompt', 'resp'), may hold values from -6 to 6
- k_resp: bfloat16 [16, 4, 1024, 128], P('prompt', None, 'resp'), may hold values from -6 to 6
- v_resp: bfloat16 [16, 4, 1024, 128], P('prompt', None, 'resp'), may hold values from -6 to 6
- dout_prefix: bfloat16 [16, 1024, 1024], P('prompt', 'resp'), may hold values from -144 to 144
- dout_resp: bfloat16 [16, 4, 1024, 1024], P('prompt', None, 'resp'), may hold values from -144 to 144
- lengths: int32 [16, 4], P('prompt'), may hold values from 1 to 1024, as said below
Outputs:
- dq_prefix: bfloat16 [16, 1024, 1024], P('prompt', 'resp')
- dq_resp: bfloat16 [16, 4, 1024, 1024], P('prompt', None, 'resp')
- dk_prefix: float32 [16, 1024, 128], P('prompt', 'resp')
- dv_prefix: float32 [16, 1024, 128], P('prompt', 'resp')
- dk_resp: float32 [16, 4, 1024, 128], P('prompt', None, 'resp')
- dv_resp: float32 [16, 4, 1024, 128], P('prompt', None, 'resp')
Inputs may be any that keep to these rules, and one draw needn't show every extreme that they name: `lengths`: some response has exactly 1024 tokens.
All inputs are finite; a program needn't handle non-finite values.
Results may differ from a plain program's by a relative error of at most 0.019.
Values may be sent and summed in bfloat16 or wider, within the bound.
No kernel may reach another device: no remote copies, remote signals or barrier semaphores. Data moves between devices by JAX's collectives and lax.ppermute only.
A program may use at most 64 MiB of HBM per device.

v0:
```python
import jax
import jax.numpy as jnp
from jax import lax
from jax.sharding import PartitionSpec as P

NEG_FILL = -1e30


def tile_grads(
    queries, douts, positions, last_pos, all_keys, all_values, key_block, grad_keys, grad_values
):
    row_count = queries.shape[0]
    head_dim = all_keys.shape[1]
    heads = queries.shape[1] // head_dim
    scale = head_dim ** (-0.5)
    flat_rows = row_count * heads
    q_flat = queries.reshape(flat_rows, head_dim)
    d_flat = douts.reshape(flat_rows, head_dim)
    row_pos = jnp.repeat(positions, heads)
    blocks = jnp.where(last_pos >= 0, last_pos // key_block + 1, 0)
    offsets = jnp.arange(key_block, dtype=jnp.int32)

    def block_scores(block_index):
        start = block_index * key_block
        key_rows = lax.dynamic_slice_in_dim(all_keys, start, key_block, 0)
        allowed = (start + offsets)[None, :] <= row_pos[:, None]
        scores = (
            jnp.einsum("rd,kd->rk", q_flat, key_rows, preferred_element_type=jnp.float32) * scale
        )
        return (start, key_rows, allowed, scores)

    def first_pass(block_index, carried):
        run_max, run_sum = carried
        start, key_rows, allowed, scores = block_scores(block_index)
        masked = jnp.where(allowed, scores, NEG_FILL)
        new_max = jnp.maximum(run_max, jnp.max(masked, axis=1))
        terms = jnp.where(allowed, jnp.exp(masked - new_max[:, None]), 0.0)
        return (new_max, run_sum * jnp.exp(run_max - new_max) + jnp.sum(terms, axis=1))

    start_max = jnp.full((flat_rows,), NEG_FILL, jnp.float32)
    run_max, run_sum = lax.fori_loop(
        0, blocks, first_pass, (start_max, jnp.zeros((flat_rows,), jnp.float32))
    )
    log_sum = run_max + jnp.log(run_sum)

    def probs_at(block_index):
        start, key_rows, allowed, scores = block_scores(block_index)
        value_rows = lax.dynamic_slice_in_dim(all_values, start, key_block, 0)
        weights = jnp.where(allowed, jnp.exp(scores - log_sum[:, None]), 0.0)
        grad_probs = jnp.einsum("rd,kd->rk", d_flat, value_rows, preferred_element_type=jnp.float32)
        return (start, key_rows, weights, grad_probs)

    def second_pass(block_index, row_delta):
        start, key_rows, weights, grad_probs = probs_at(block_index)
        return row_delta + jnp.sum(weights * grad_probs, axis=1)

    row_delta = lax.fori_loop(0, blocks, second_pass, jnp.zeros((flat_rows,), jnp.float32))

    def third_pass(block_index, carried):
        grad_q, acc_keys, acc_values = carried
        start, key_rows, weights, grad_probs = probs_at(block_index)
        weights_low = weights.astype(jnp.bfloat16)
        value_part = jnp.einsum(
            "rk,rd->kd", weights_low, d_flat, preferred_element_type=jnp.float32
        )
        grad_scores = (weights * (grad_probs - row_delta[:, None])).astype(jnp.bfloat16)
        grad_q = grad_q + jnp.dot(grad_scores, key_rows, preferred_element_type=jnp.float32)
        key_part = (
            jnp.einsum("rk,rd->kd", grad_scores, q_flat, preferred_element_type=jnp.float32) * scale
        )
        old_keys = lax.dynamic_slice_in_dim(acc_keys, start, key_block, 0)
        old_values = lax.dynamic_slice_in_dim(acc_values, start, key_block, 0)
        acc_keys = lax.dynamic_update_slice_in_dim(acc_keys, old_keys + key_part, start, 0)
        acc_values = lax.dynamic_update_slice_in_dim(acc_values, old_values + value_part, start, 0)
        return (grad_q, acc_keys, acc_values)

    start_q = jnp.zeros((flat_rows, head_dim), jnp.float32)
    grad_q, grad_keys, grad_values = lax.fori_loop(
        0, blocks, third_pass, (start_q, grad_keys, grad_values)
    )
    return ((grad_q * scale).reshape(row_count, heads * head_dim), grad_keys, grad_values)


def rows_grads(
    queries, douts, first_pos, last_live, all_keys, all_values, key_block, grad_keys, grad_values
):
    row_count = queries.shape[0]
    heads = queries.shape[1] // all_keys.shape[1]
    piece_rows = min(row_count, max(1, 512 // heads))
    begin_pos = first_pos + 0
    positions = begin_pos + jnp.arange(piece_rows, dtype=jnp.int32)
    last_pos = jnp.where(
        begin_pos <= last_live, jnp.minimum(begin_pos + piece_rows - 1, last_live), -1
    )
    grad_q, grad_keys, grad_values = tile_grads(
        queries, douts, positions, last_pos, all_keys, all_values, key_block, grad_keys, grad_values
    )
    return (grad_q, grad_keys, grad_values)


def per_device(
    q_prefix, q_resp, k_prefix, v_prefix, k_resp, v_resp, dout_prefix, dout_resp, lengths
):
    count_local = jnp.sum(lengths[0].astype(jnp.float32))
    total = lax.psum(count_local, "prompt")
    prefix_keys, prefix_values = (
        lax.all_gather(k_prefix[0], "resp", axis=0, tiled=True),
        lax.all_gather(v_prefix[0], "resp", axis=0, tiled=True),
    )
    own_keys, own_values = (
        lax.all_gather(k_resp[0], "resp", axis=1, tiled=True),
        lax.all_gather(v_resp[0], "resp", axis=1, tiled=True),
    )
    prefix_len = prefix_keys.shape[0]
    resp_count = own_keys.shape[0]
    resp_len = own_keys.shape[1]
    token_scale = jnp.float32(lax.axis_size("prompt") * resp_count * resp_len) / (2.0 * total)
    key_block = min(512, prefix_len, resp_len)
    my_index = lax.axis_index("resp")
    prefix_rows_dev = q_prefix.shape[1]
    prefix_first = my_index * prefix_rows_dev
    cot_prefix = (dout_prefix[0].astype(jnp.float32) * token_scale).astype(jnp.bfloat16)
    prefix_empty = jnp.zeros(prefix_keys.shape, jnp.float32)
    dq_self, prefix_dk, prefix_dv = rows_grads(
        q_prefix[0],
        cot_prefix,
        prefix_first,
        prefix_first + prefix_rows_dev - 1,
        prefix_keys,
        prefix_values,
        key_block,
        prefix_empty,
        prefix_empty,
    )
    part_rows = q_resp.shape[2]
    local_pos = my_index * part_rows + jnp.arange(part_rows, dtype=jnp.int32)
    scaled = (dout_resp[0].astype(jnp.float32) * token_scale).astype(jnp.bfloat16)
    is_live = (local_pos[None, :] < lengths[0][:, None])[:, :, None]
    cot_resp = jnp.where(is_live, scaled, jnp.zeros_like(scaled))
    own_first = prefix_len + my_index * part_rows
    own_parts = []
    key_parts = []
    value_parts = []
    for index in range(resp_count):
        all_keys = jnp.concatenate([prefix_keys, own_keys[index]], axis=0)
        all_values = jnp.concatenate([prefix_values, own_values[index]], axis=0)
        last_live = prefix_len + lengths[0, index] - 1
        empty_acc = jnp.zeros(all_keys.shape, jnp.float32)
        dq_own, grad_keys, grad_values = rows_grads(
            q_resp[0, index],
            cot_resp[index],
            own_first,
            last_live,
            all_keys,
            all_values,
            key_block,
            empty_acc,
            empty_acc,
        )
        own_parts.append(dq_own.astype(jnp.bfloat16))
        prefix_dk = prefix_dk + grad_keys[:prefix_len]
        prefix_dv = prefix_dv + grad_values[:prefix_len]
        key_parts.append(grad_keys[prefix_len:])
        value_parts.append(grad_values[prefix_len:])
    dq_rows = jnp.stack(own_parts, axis=0)
    resp_dk = jnp.stack(key_parts, axis=0)
    resp_dv = jnp.stack(value_parts, axis=0)
    dk_prefix, dv_prefix = (
        lax.psum_scatter(
            prefix_dk.astype(jnp.bfloat16), "resp", scatter_dimension=0, tiled=True
        ).astype(jnp.float32),
        lax.psum_scatter(
            prefix_dv.astype(jnp.bfloat16), "resp", scatter_dimension=0, tiled=True
        ).astype(jnp.float32),
    )
    dk_resp, dv_resp = (
        lax.psum_scatter(
            resp_dk.astype(jnp.bfloat16), "resp", scatter_dimension=1, tiled=True
        ).astype(jnp.float32),
        lax.psum_scatter(
            resp_dv.astype(jnp.bfloat16), "resp", scatter_dimension=1, tiled=True
        ).astype(jnp.float32),
    )
    return (
        dq_self.astype(jnp.bfloat16)[None],
        dq_rows[None],
        dk_prefix[None],
        dv_prefix[None],
        dk_resp[None],
        dv_resp[None],
    )


def solution(mesh):
    placed = (
        P("prompt", "resp", None),
        P("prompt", None, "resp", None),
        P("prompt", "resp", None),
        P("prompt", "resp", None),
        P("prompt", None, "resp", None),
        P("prompt", None, "resp", None),
        P("prompt", "resp", None),
        P("prompt", None, "resp", None),
        P("prompt", None),
    )
    return jax.shard_map(
        per_device,
        mesh=mesh,
        in_specs=placed,
        out_specs=(
            P("prompt", "resp", None),
            P("prompt", None, "resp", None),
            P("prompt", "resp", None),
            P("prompt", "resp", None),
            P("prompt", None, "resp", None),
            P("prompt", None, "resp", None),
        ),
        check_vma=False,
    )
```

profile of v0, /device:TPU:16, one launch (start us, length us, event | category | flops | bytes accessed | tf_op | source)
XLA Modules:
  0.0 585.2 jit_solution(6859271114077419288)
XLA Ops:
  13.9 38.3 %all-gather = bf16[1,1024,128]{2,1,0:T(8,128)(2,1)S(1)} all-gather(bf16[1,64,128]{2,1,0:T(8,128)(2,1)S(1)} %copy-done.14), channel_id=2, replica_groups=mesh['prompt'=16,'resp'=16] {'resp'}, dimensions={1}, use_global_device_ids=true | all-gather | bytes 278528 | tf_op jit(solution)/shard_map/all_gather | solution.py:107
  53.1 31.9 %all-gather.1 = bf16[1,1024,128]{2,1,0:T(8,128)(2,1)S(1)} all-gather(bf16[1,64,128]{2,1,0:T(8,128)(2,1)S(1)} %copy-done.15), channel_id=3, replica_groups=mesh['prompt'=16,'resp'=16] {'resp'}, dimensions={1}, use_global_device_ids=true | all-gather | bytes 278528 | tf_op jit(solution)/shard_map/all_gather | solution.py:108
  85.0 29.1 %psum.7 = f32[]{:T(128)} all-reduce(f32[]{:T(128)} %convert_reduce_fusion), channel_id=1, replica_groups=mesh['prompt'=16,'resp'=16] {'prompt'}, use_global_device_ids=true, to_apply=%region_5.6 | all-reduce | flops 1 | bytes 8 | tf_op jit(solution)/shard_map/psum | solution.py:105
  116.0 1.9 while.197
  121.9 1.3 pad_maximum_fusion.5
  123.3 2.4 while.207
  125.7 25.3 %all-gather.9.cloned.1.call-done = bf16[1,4,1024,128]{3,2,1,0:T(8,128)(2,1)} async-done(((bf16[1,4,64,128]{3,2,1,0:T(8,128)(2,1)}), bf16[1,4,1024,128]{3,2,1,0:T(8,128)(2,1)}) %all-gather.9.cloned.1.call-update) | async-done | bytes 1048592 | tf_op jit(solution)/shard_map/all_gather | solution.py:112
  152.2 1.4 pad_maximum_fusion.9
  153.6 2.7 while.208
  158.5 26.6 %while.209 = (s32[]{:T(128)}, f32[512,128]{1,0:T(8,128)S(1)}, f32[2048,128]{1,0:T(8,128)}, f32[2048,128]{1,0:T(8,128)S(1)}, s32[]{:T(128)}, /*index=5*/bf16[2048...) while((s32[]{:T(128)}, f32[512,128]{1,0:T(8,128)S(1)}, ...), condition=%wide.region_46.47_spmd.clone, body=%wide.region_45.46_spmd.clone.sunk | while | flops 337904128 | bytes 7242267 | solution.py:78
  160.6 1.3 fusion.509
  164.4 2.0 fusion.511
  169.5 1.3 fusion.509
  173.3 2.0 fusion.511
  178.4 1.3 fusion.509
  182.1 1.9 fusion.511
  186.0 5.1 while.204
  191.2 8.2 %while.205 = (s32[]{:T(128)}, f32[512]{0:T(512)S(1)}, s32[]{:T(128)}, bf16[2048,128]{1,0:T(8,128)(2,1)}, bf16[512,128]{1,0:T(8,128)(2,1)S(1)}, /*index=5*/f32[51...) while((s32[]{:T(128)}, f32[512]{0:T(512)S(1)}, ...), condition=%wide.region_35.36_spmd.clone, body=%wide.region_33.35_spmd.clone.sunk | while | flops 135791104 | bytes 2644415 | solution.py:57
  196.9 1.3 fusion.474
  201.8 23.2 %while.206 = (s32[]{:T(128)}, f32[512,128]{1,0:T(8,128)S(1)}, f32[2048,128]{1,0:T(8,128)}, f32[2048,128]{1,0:T(8,128)S(1)}, s32[]{:T(128)}, /*index=5*/bf16[2048...) while((s32[]{:T(128)}, f32[512,128]{1,0:T(8,128)S(1)}, ...), condition=%wide.region_37.38_spmd.clone, body=%wide.region_36.37_spmd.clone.sunk | while | flops 337904128 | bytes 7750143 | solution.py:78
  203.4 1.3 fusion.486
  206.0 1.3 convolution_add_fusion.18
  207.3 1.9 fusion.488
  211.1 1.4 fusion.486
  213.7 1.3 convolution_add_fusion.18
  215.0 2.0 fusion.488
  218.9 1.4 fusion.486
  221.4 1.3 convolution_add_fusion.18
  222.8 2.0 fusion.488
  226.1 5.1 while.201
  231.2 8.4 %while.202 = (s32[]{:T(128)}, f32[512]{0:T(512)S(1)}, s32[]{:T(128)}, bf16[2048,128]{1,0:T(8,128)(2,1)}, bf16[512,128]{1,0:T(8,128)(2,1)S(1)}, /*index=5*/f32[51...) while((s32[]{:T(128)}, f32[512]{0:T(512)S(1)}, ...), condition=%wide.region_26.27_spmd.clone, body=%wide.region_24.26_spmd.clone.sunk | while | flops 135791104 | bytes 2644415 | solution.py:57
  231.6 1.3 fusion.451
  242.0 23.2 %while.203 = (s32[]{:T(128)}, f32[512,128]{1,0:T(8,128)S(1)}, f32[2048,128]{1,0:T(8,128)}, f32[2048,128]{1,0:T(8,128)S(1)}, s32[]{:T(128)}, /*index=5*/bf16[2048...) while((s32[]{:T(128)}, f32[512,128]{1,0:T(8,128)S(1)}, ...), condition=%wide.region_28.29_spmd.clone, body=%wide.region_27.28_spmd.clone.sunk | while | flops 337904128 | bytes 7750143 | solution.py:78
  243.6 1.4 fusion.463
  246.2 1.3 convolution_add_fusion.17
  247.5 1.9 fusion.465
  251.3 1.4 fusion.463
  253.9 1.3 convolution_add_fusion.17
  255.2 1.9 fusion.465
  259.0 1.4 fusion.463
  261.6 1.3 convolution_add_fusion.17
  262.9 1.9 fusion.465
  266.2 5.1 while.198
  271.3 8.2 %while.199 = (s32[]{:T(128)}, f32[512]{0:T(512)S(1)}, s32[]{:T(128)}, bf16[2048,128]{1,0:T(8,128)(2,1)}, bf16[512,128]{1,0:T(8,128)(2,1)S(1)}, /*index=5*/f32[51...) while((s32[]{:T(128)}, f32[512]{0:T(512)S(1)}, ...), condition=%wide.region_17.18_spmd.clone, body=%wide.region_15.17_spmd.clone.sunk | while | flops 135791104 | bytes 2644415 | solution.py:57
  271.5 1.3 fusion.428
  274.3 1.3 fusion.428
  277.0 1.3 fusion.428
  281.8 18.2 %while.200 = (s32[]{:T(128)}, f32[512,128]{1,0:T(8,128)S(1)}, f32[2048,128]{1,0:T(8,128)}, f32[2048,128]{1,0:T(8,128)}, s32[]{:T(128)}, /*index=5*/bf16[2048,128...) while((s32[]{:T(128)}, f32[512,128]{1,0:T(8,128)S(1)}, ...), condition=%wide.region_19.20_spmd.clone, body=%wide.region_18.19_spmd.clone.sunk | while | flops 337904128 | bytes 7225827 | solution.py:78
  284.0 1.9 fusion.442
  285.9 2.0 fusion.443
  290.1 1.9 fusion.442
  292.0 2.0 fusion.443
  296.1 1.9 fusion.442
  298.1 2.0 fusion.443
  300.0 2.4 add_convert_fusion.1
  302.5 2.3 add_convert_fusion
  314.3 54.1 %reduce-scatter.5.cloned.1.call-done = bf16[64,128]{1,0:T(8,128)(2,1)} async-done(((bf16[1024,128]{1,0:T(8,128)(2,1)}), bf16[64,128]{1,0:T(8,128)(2,1)}) %reduce-scatter.5.cloned.1.call-update) | async-done | bytes 16400 | tf_op jit(solution)/shard_map/reduce_scatter | solution.py:169
  368.4 1.3 bitcast_convert_fusion.3
  369.7 67.0 %reduce-scatter.7.cloned.1.call-done = bf16[64,128]{1,0:T(8,128)(2,1)} async-done(((bf16[1024,128]{1,0:T(8,128)(2,1)}), bf16[64,128]{1,0:T(8,128)(2,1)}) %reduce-scatter.7.cloned.1.call-update) | async-done | bytes 16400 | tf_op jit(solution)/shard_map/reduce_scatter | solution.py:172
  436.8 1.3 bitcast_convert_fusion.2
  438.1 68.5 %reduce-scatter.9.cloned.1.call-done = bf16[4,64,128]{2,1,0:T(8,128)(2,1)} async-done(((bf16[4,1024,128]{2,1,0:T(8,128)(2,1)}), bf16[4,64,128]{2,1,0:T(8,128)(2,1)}) %reduce-scatter.9.cloned.1.call-update) | async-done | bytes 65552 | tf_op jit(solution)/shard_map/reduce_scatter | solution.py:177
  506.6 1.5 bitcast_convert_fusion.1
  508.1 68.7 %reduce-scatter.11.cloned.1.call-done = bf16[4,64,128]{2,1,0:T(8,128)(2,1)} async-done(((bf16[4,1024,128]{2,1,0:T(8,128)(2,1)}), bf16[4,64,128]{2,1,0:T(8,128)(2,1)}) %reduce-scatter.11.cloned.1.call-update) | async-done | bytes 65552 | tf_op jit(solution)/shard_map/reduce_scatter | solution.py:180
  576.8 1.5 bitcast_convert_fusion
  (397 shorter events, 115.0 us)
Async XLA Ops:
  7.2 113.5 %all-gather.7.cloned.1.call-start = ((), (), s32[]{:S(2)}) async-start(), calls=%async_computation.8 | async-start | bytes 1114112 | tf_op jit(solution)/shard_map/all_gather | solution.py:111
  7.9 143.0 %all-gather.9.cloned.1.call-start = ((), (), s32[]{:S(2)}) async-start(), calls=%async_computation.9 | async-start | bytes 1114112 | tf_op jit(solution)/shard_map/all_gather | solution.py:112
  8.6 359.8 %reduce-scatter.5.cloned.1.call-start = ((), (), s32[]{:S(2)}) async-start(), calls=%async_computation.4 | async-start | bytes 278528 | tf_op jit(solution)/shard_map/reduce_scatter | solution.py:169
  8.7 0.7 copy-start.16
  13.1 0.7 copy-start.14
  13.9 38.3 %copy-start.12 = (bf16[1,64,1024]{2,1,0:T(8,128)(2,1)S(1)}, bf16[1,64,1024]{2,1,0:T(8,128)(2,1)}, u32[]{:S(2)}) copy-start(bf16[1,64,1024]{2,1,0:T(8,128)(2,1)} %param.39) | copy-start | bytes 393220
  52.2 0.8 copy-start.15
  53.1 61.7 %copy-start.13 = (bf16[1,64,1024]{2,1,0:T(8,128)(2,1)S(1)}, bf16[1,64,1024]{2,1,0:T(8,128)(2,1)}, u32[]{:S(2)}) copy-start(bf16[1,64,1024]{2,1,0:T(8,128)(2,1)} %param.45) | copy-start | bytes 393220
  117.9 1.4 copy-start.11
  156.3 0.8 copy-start.3
  156.4 1.0 copy-start.10
  158.5 0.6 copy-start.17
  166.7 0.7 copy-start.18
  167.4 0.6 copy-start.17
  175.5 0.7 copy-start.18
  176.2 0.6 copy-start.17
  184.4 0.7 copy-start.18
  185.1 1.0 copy-start
  199.4 0.7 copy-start.7
  200.1 0.6 copy-start.19
  201.8 23.3 %copy-start.4 = (bf16[512,128]{1,0:T(8,128)(2,1)S(1)}, bf16[512,128]{1,0:T(8,128)(2,1)}, u32[]{:S(2)}) copy-start(bf16[512,128]{1,0:T(8,128)(2,1)} %reshape_squeeze.30) | copy-start | bytes 393220
  206.0 1.3 copy-start.8
  213.7 1.3 copy-start.8
  221.4 1.3 copy-start.8
  225.0 1.0 copy-start.1
  239.6 0.7 copy-start.5
  240.3 0.6 copy-start.20
  246.1 1.3 copy-start.6
  253.9 1.3 copy-start.6
  261.6 1.3 copy-start.6
  265.2 1.0 copy-start.2
  280.6 1.2 copy-start.9
  302.4 134.3 %reduce-scatter.7.cloned.1.call-start = ((), (), s32[]{:S(2)}) async-start(), calls=%async_computation.5 | async-start | bytes 278528 | tf_op jit(solution)/shard_map/reduce_scatter | solution.py:172
  304.8 201.8 %reduce-scatter.9.cloned.1.call-start = ((), (), s32[]{:S(2)}) async-start(), calls=%async_computation.6 | async-start | bytes 1114112 | tf_op jit(solution)/shard_map/reduce_scatter | solution.py:177
  308.6 268.3 %reduce-scatter.11.cloned.1.call-start = ((), (), s32[]{:S(2)}) async-start(), calls=%async_computation.7 | async-start | bytes 1114112 | tf_op jit(solution)/shard_map/reduce_scatter | solution.py:180
Sparse Core Ops, SparseCore 0:
  9.8 72.1 all-gather.6
  83.8 67.1 all-gather.8
  302.5 65.8 reduce-scatter.4
  370.9 65.7 reduce-scatter.6
  439.1 67.4 reduce-scatter.8
  509.1 67.6 reduce-scatter.10
where the time goes:
time: 588 us; the launch traced here: 585 us
  waiting for transfers between devices  285 us (48%)
  matrix products  112 us (19%)
  blocking collectives  99.3 us (17%)
  local copies, waits for them, and re-layouts  47.8 us (8%)
  other arithmetic  20.8 us (4%)
  between operations  18.1 us (3%)
    reduce_scatter x1, waiting for transfers between devices, per_device(): lax.psum_scatter(resp_dv.astype(jnp.bfloat16), 'resp', scatter_dimension=...  68.7 us
    reduce_scatter x1, waiting for transfers between devices, per_device(): lax.psum_scatter(resp_dk.astype(jnp.bfloat16), 'resp', scatter_dimension=...  68.5 us
    reduce_scatter x1, waiting for transfers between devices, per_device(): lax.psum_scatter(prefix_dv.astype(jnp.bfloat16), 'resp', scatter_dimensio...  67 us
    reduce_scatter x1, waiting for transfers between devices, per_device(): lax.psum_scatter(prefix_dk.astype(jnp.bfloat16), 'resp', scatter_dimensio...  54.1 us
    dot_general x39, matrix products, block_scores(): jnp.einsum('rd,kd->rk', q_flat, key_rows, preferred_element_type=jnp.floa...  38.9 us
    all_gather x1, blocking collectives, per_device(): lax.all_gather(k_prefix[0], 'resp', axis=0, tiled=True)  38.3 us
    all_gather x1, blocking collectives, per_device(): lax.all_gather(v_prefix[0], 'resp', axis=0, tiled=True)  31.9 us
    psum x1, blocking collectives, per_device(): total = lax.psum(count_local, 'prompt')  29.1 us
  transfers between devices with their start and end apart: 6, of which 5 were waited for; matrix products, arithmetic and copies ran while one was open for 5% of the time, Pallas kernels for 0%

commit v1 on v0

v1 whole, which is shorter than its diff:
```python
import functools

import jax
import jax.numpy as jnp
from jax import lax
from jax.experimental import pallas as pl
from jax.experimental.pallas import tpu as pltpu
from jax.sharding import PartitionSpec as P

HD = 128
HEADS = 8
ROWS = 64
CHUNK = ROWS * HEADS
ZN = 8
NEG = -1e30
SCALE = HD**-0.5
LOG2E = 1.4426950408889634
TILE_BLOCKS = 4
TILE = TILE_BLOCKS * ROWS
VMEM = pl.BlockSpec(memory_space=pltpu.VMEM)
SMEM = pl.BlockSpec(memory_space=pltpu.SMEM)
F32 = jnp.float32
BF16 = jnp.bfloat16


def dot_nt(a, b):
    return lax.dot_general(a, b, (((1,), (1,)), ((), ())), preferred_element_type=F32)


def dot_tn(a, b):
    return lax.dot_general(a, b, (((0,), (0,)), ((), ())), preferred_element_type=F32)


def dot_nn(a, b):
    return lax.dot_general(a, b, (((1,), (0,)), ((), ())), preferred_element_type=F32)


def stack_heads(rows):
    return jnp.concatenate([rows[:, h * HD : (h + 1) * HD] for h in range(HEADS)], axis=0)


def unstack_heads(rows):
    return jnp.concatenate([rows[h * ROWS : (h + 1) * ROWS] for h in range(HEADS)], axis=1)


def keep_mask(key_first, row_first, tile):
    key_pos = key_first + lax.broadcasted_iota(jnp.int32, (tile, CHUNK), 0)
    row_pos = row_first + (lax.broadcasted_iota(jnp.int32, (tile, CHUNK), 1) & (ROWS - 1))
    return key_pos <= row_pos


def stats_step(stats, q, d, kt, vt, keep):
    top, total, mixed = stats
    s = dot_nt(kt, q) * (SCALE * LOG2E)
    g = dot_nt(vt, d)
    if keep is not None:
        s = jnp.where(keep, s, NEG)
    new_top = jnp.maximum(top, jnp.max(s, axis=0, keepdims=True))
    e = jnp.exp2(s - new_top)
    fix = jnp.exp2(top - new_top)
    total = total * fix + jnp.sum(e, axis=0, keepdims=True)
    mixed = mixed * fix + jnp.sum(e * g, axis=0, keepdims=True)
    return new_top, total, mixed


def grads_step(q, d, kt, vt, log_sum, delta, keep):
    s = dot_nt(kt, q) * (SCALE * LOG2E)
    g = dot_nt(vt, d)
    w = jnp.exp2(s - log_sum)
    if keep is not None:
        w = jnp.where(keep, w, 0.0)
    grad_s = (w * (g - delta)).astype(BF16)
    dv = dot_nn(w.astype(BF16), d)
    dk = dot_nn(grad_s, q)
    dq = dot_tn(grad_s, kt)
    return dq, dk, dv


def empty_stats():
    return (
        jnp.full((1, CHUNK), NEG, F32),
        jnp.zeros((1, CHUNK), F32),
        jnp.zeros((1, CHUNK), F32),
    )


def finish(stats):
    top, total, mixed = stats
    return top + jnp.log2(total), mixed / total


def tile_of(ref, lead, first, kind):
    return ref[lead, pl.ds(first, TILE_BLOCKS), kind].reshape(TILE, HD)


def chunk_first(info, chunk):
    half = info[0] ^ (chunk & 1)
    return (half * ZN + info[1]) * ROWS


def chunk_length(info, chunk):
    return info[2 + (chunk >> 1)]


def prefix_kernel(
    info, qr, dr, got, qp, dp, kv_own, kv_pair,
    q_st, d_st, stats_out, dq_out, acc, kv, q1, d1, dq_acc,
):
    half = info[0]
    z = info[1]
    kv[half] = kv_own[...]
    kv[1 - half] = kv_pair[...]
    acc[...] = jnp.zeros_like(acc)
    q1[...] = stack_heads(qp[0])
    d1[...] = stack_heads(dp[0])
    dq_acc[...] = jnp.zeros_like(dq_acc)
    block = half * ZN + z
    tiles = block // TILE_BLOCKS + 1

    def load(tile):
        lead = tile // 2
        first = (tile % 2) * TILE_BLOCKS
        keep = keep_mask(tile * TILE, block * ROWS, TILE)
        return lead, first, keep

    def first_pass(tile, stats):
        lead, first, keep = load(tile)
        return stats_step(
            stats, q1[...], d1[...], tile_of(kv, lead, first, 0), tile_of(kv, lead, first, 1), keep
        )

    log_sum, delta = finish(lax.fori_loop(0, tiles, first_pass, empty_stats()))

    def second_pass(tile, carried):
        lead, first, keep = load(tile)
        dq, dk, dv = grads_step(
            q1[...], d1[...], tile_of(kv, lead, first, 0), tile_of(kv, lead, first, 1),
            log_sum, delta, keep,
        )
        dq_acc[...] += dq
        acc[lead, pl.ds(first, TILE_BLOCKS), 0] += dk.reshape(TILE_BLOCKS, ROWS, HD)
        acc[lead, pl.ds(first, TILE_BLOCKS), 1] += dv.reshape(TILE_BLOCKS, ROWS, HD)
        return carried

    lax.fori_loop(0, tiles, second_pass, 0)
    dq_out[...] = unstack_heads(dq_acc[...])
    for chunk in range(4):
        resp = chunk >> 1
        if chunk & 1:
            queries, douts = got[0, resp], got[1, resp]
        else:
            queries, douts = qr[0, 2 * half + resp], dr[0, 2 * half + resp]
        pos = chunk_first(info, chunk) + lax.broadcasted_iota(jnp.int32, douts.shape, 0)
        douts = jnp.where(pos < chunk_length(info, chunk), douts.astype(F32), 0.0).astype(BF16)
        q_st[chunk] = stack_heads(queries)
        d_st[chunk] = stack_heads(douts)

    def one_chunk(chunk, carried):
        @pl.when(chunk_first(info, chunk) < chunk_length(info, chunk))
        def _():
            stats = empty_stats()
            for lead in range(2):
                for first in range(0, ZN, TILE_BLOCKS):
                    stats = stats_step(
                        stats, q_st[chunk], d_st[chunk],
                        tile_of(kv, lead, first, 0), tile_of(kv, lead, first, 1), None,
                    )
            for row in range(3):
                stats_out[chunk, row : row + 1] = stats[row]

        return carried

    lax.fori_loop(0, 4, one_chunk, 0)


def resp_kernel(info, q_st, d_st, stats_in, kv, log_out, dq_out, grads, acc):
    half = info[0]
    acc[...] = jnp.zeros_like(acc)
    dq_out[...] = jnp.zeros_like(dq_out)

    def one_chunk(chunk, carried):
        @pl.when(chunk_first(info, chunk) < chunk_length(info, chunk))
        def _():
            resp = chunk >> 1
            row_first = chunk_first(info, chunk)
            tiles = row_first // TILE + 1

            def load(tile):
                slot = (tile // 2) ^ half
                first = (tile % 2) * TILE_BLOCKS
                keys = kv[pl.ds(first, TILE_BLOCKS), slot, 0, resp].reshape(TILE, HD)
                values = kv[pl.ds(first, TILE_BLOCKS), slot, 1, resp].reshape(TILE, HD)
                return slot, first, keys, values, keep_mask(tile * TILE, row_first, TILE)

            def first_pass(tile, stats):
                slot, first, keys, values, keep = load(tile)
                return stats_step(stats, q_st[chunk], d_st[chunk], keys, values, keep)

            begin = tuple(stats_in[chunk, row : row + 1] for row in range(3))
            log_sum, delta = finish(lax.fori_loop(0, tiles, first_pass, begin))
            log_out[chunk, 0:1] = log_sum
            log_out[chunk, 1:2] = delta

            def second_pass(tile, inner):
                slot, first, keys, values, keep = load(tile)
                dq, dk, dv = grads_step(
                    q_st[chunk], d_st[chunk], keys, values, log_sum, delta, keep
                )
                dq_out[chunk] += dq
                acc[pl.ds(first, TILE_BLOCKS), slot, 0, resp] += dk.reshape(TILE_BLOCKS, ROWS, HD)
                acc[pl.ds(first, TILE_BLOCKS), slot, 1, resp] += dv.reshape(TILE_BLOCKS, ROWS, HD)
                return inner

            lax.fori_loop(0, tiles, second_pass, 0)

        return carried

    lax.fori_loop(0, 4, one_chunk, 0)
    grads[...] = acc[...].astype(BF16)


def final_kernel(
    info, token_scale, q_st, d_st, logs, dq_in, dqp_in, kv_own, kv_pair, acc_in,
    dqp_out, dq_own, dq_pair, g_own, g_pair, dq_acc, acc,
):
    half = info[0]
    factor = token_scale[0] * SCALE
    dqp_out[0] = (dqp_in[...] * factor).astype(BF16)
    acc[0] = acc_in[half]
    acc[1] = acc_in[1 - half]
    dq_acc[...] = dq_in[...]

    def one_chunk(chunk, carried):
        @pl.when(chunk_first(info, chunk) < chunk_length(info, chunk))
        def _():
            log_sum = logs[chunk, 0:1]
            delta = logs[chunk, 1:2]
            for lead, kv in enumerate((kv_own, kv_pair)):
                for first in range(0, ZN, TILE_BLOCKS):
                    keys = kv[pl.ds(first, TILE_BLOCKS), 0].reshape(TILE, HD)
                    values = kv[pl.ds(first, TILE_BLOCKS), 1].reshape(TILE, HD)
                    dq, dk, dv = grads_step(
                        q_st[chunk], d_st[chunk], keys, values, log_sum, delta, None
                    )
                    dq_acc[chunk] += dq
                    acc[lead, pl.ds(first, TILE_BLOCKS), 0] += dk.reshape(TILE_BLOCKS, ROWS, HD)
                    acc[lead, pl.ds(first, TILE_BLOCKS), 1] += dv.reshape(TILE_BLOCKS, ROWS, HD)

        return carried

    lax.fori_loop(0, 4, one_chunk, 0)
    for resp in range(2):
        dq_own[resp] = unstack_heads((dq_acc[2 * resp] * factor).astype(BF16))
        dq_pair[resp] = unstack_heads((dq_acc[2 * resp + 1] * factor).astype(BF16))
    g_own[...] = acc[0]
    g_pair[...] = acc[1].astype(BF16)


def shape(dims, dtype):
    return jax.ShapeDtypeStruct(dims, dtype)


def call(kernel, ins, outs, scratch, flops, smem):
    return pl.pallas_call(
        kernel,
        out_shape=outs,
        in_specs=[SMEM] * smem + [VMEM] * (ins - smem),
        out_specs=[VMEM] * len(outs),
        scratch_shapes=scratch,
        cost_estimate=pl.CostEstimate(flops=flops, bytes_accessed=4 << 20, transcendentals=0),
        compiler_params=pltpu.CompilerParams(vmem_limit_bytes=48 << 20),
    )


def per_device(
    q_prefix, q_resp, k_prefix, v_prefix, k_resp, v_resp, dout_prefix, dout_resp, lengths
):
    me = lax.axis_index("resp")
    half, z = me // ZN, me % ZN
    pair = [(i, (i + ZN) % (2 * ZN)) for i in range(2 * ZN)]
    columns = [list(range(ZN)), list(range(ZN, 2 * ZN))]

    def swap(value):
        return lax.ppermute(value, "resp", pair)

    def spread(value):
        return lax.all_to_all(value, "resp", 0, 0, axis_index_groups=columns)

    def mine(value):
        return lax.dynamic_slice_in_dim(value, 2 * half, 2, 0)

    def theirs(value):
        return lax.dynamic_slice_in_dim(value, 2 * (1 - half), 2, 0)

    pre = jnp.stack([k_prefix[0], v_prefix[0]])
    kvp_own = spread(jnp.broadcast_to(pre[None], (ZN,) + pre.shape))
    kv_sent = jnp.stack([theirs(k_resp[0]), theirs(v_resp[0])])
    kv_got = swap(kv_sent)
    kv_mine = jnp.stack([mine(k_resp[0]), mine(v_resp[0])])
    block = jnp.stack([kv_mine, kv_got])
    got = swap(jnp.stack([theirs(q_resp[0]), theirs(dout_resp[0])]))
    kvr = spread(jnp.broadcast_to(block[None], (ZN,) + block.shape))
    kvp_pair = swap(kvp_own)

    count = jnp.sum(lengths[0].astype(F32))
    count = jnp.broadcast_to(count, (8, HD))
    for step in (1, 2, 4, 8):
        count = count + lax.ppermute(count, "prompt", [(i, i ^ step) for i in range(16)])
    token_scale = (F32(65536.0) / (2.0 * count[0, :1]))

    info = jnp.concatenate([jnp.stack([half, z]).astype(jnp.int32), mine(lengths[0])])
    st = shape((4, CHUNK, HD), BF16)
    q_st, d_st, stats, dqp, acc_p = call(
        prefix_kernel, 8,
        [st, st, shape((4, 8, CHUNK), F32), shape((ROWS, HEADS * HD), F32),
         shape((2, ZN, 2, ROWS, HD), F32)],
        [pltpu.VMEM((2, ZN, 2, ROWS, HD), BF16), pltpu.VMEM((CHUNK, HD), BF16),
         pltpu.VMEM((CHUNK, HD), BF16), pltpu.VMEM((CHUNK, HD), F32)],
        3 << 30, 1,
    )(info, q_resp, dout_resp, got, q_prefix, dout_prefix, kvp_own, kvp_pair)
    logs, dq_part, grads_r = call(
        resp_kernel, 5,
        [shape((4, 8, CHUNK), F32), shape((4, CHUNK, HD), F32),
         shape((ZN, 2, 2, 2, ROWS, HD), BF16)],
        [pltpu.VMEM((ZN, 2, 2, 2, ROWS, HD), F32)],
        3 << 30, 1,
    )(info, q_st, d_st, stats, kvr)
    terms_r = spread(grads_r)
    dqp_out, dq_own, dq_pair, g_own, g_pair = call(
        final_kernel, 10,
        [shape((1, ROWS, HEADS * HD), BF16), shape((2, ROWS, HEADS * HD), BF16),
         shape((2, ROWS, HEADS * HD), BF16), shape((ZN, 2, ROWS, HD), F32),
         shape((ZN, 2, ROWS, HD), BF16)],
        [pltpu.VMEM((4, CHUNK, HD), F32), pltpu.VMEM((2, ZN, 2, ROWS, HD), F32)],
        4 << 30, 2,
    )(info, token_scale, q_st, d_st, logs, dq_part, dqp, kvp_own, kvp_pair, acc_p)

    g_sum = (g_own + swap(g_pair).astype(F32)).astype(BF16)
    dq_got = swap(dq_pair)
    terms_p = spread(g_sum)
    kinds = jnp.stack([token_scale * F32(SCALE), token_scale])[:, :, None]
    sum_p = jnp.sum(terms_p.astype(F32), axis=0) * kinds
    sum_r = jnp.sum(terms_r.astype(F32), axis=0) * kinds[None, :, :, :, None]
    back = swap(sum_r[1].astype(BF16)).astype(F32)
    first_half = half == 0

    def arrange(own, other):
        return jnp.where(
            first_half, jnp.concatenate([own, other]), jnp.concatenate([other, own])
        )[None]

    return (
        dqp_out,
        arrange(dq_own, dq_got),
        sum_p[0][None],
        sum_p[1][None],
        arrange(sum_r[0, 0], back[0]),
        arrange(sum_r[0, 1], back[1]),
    )


def solution(mesh):
    rows = P("prompt", "resp", None)
    resp_rows = P("prompt", None, "resp", None)
    return jax.shard_map(
        per_device,
        mesh=mesh,
        in_specs=(
            rows, resp_rows, rows, rows, resp_rows, resp_rows, rows, resp_rows, P("prompt", None),
        ),
        out_specs=(rows, resp_rows, rows, rows, resp_rows, resp_rows),
        check_vma=False,
    )
```

time: 588 us -> 148 us (0.25)
  waiting for transfers between devices: 285 us -> 65.5 us
  matrix products: 112 us -> 0 us
  blocking collectives: 99.3 us -> 15.2 us
  local copies, waits for them, and re-layouts: 47.8 us -> 10.7 us
  starting transfers between devices: 0.24 us -> 34.7 us
  between operations: 18.1 us -> 2.2 us
  other arithmetic: 20.8 us -> 6.33 us
  Pallas kernels: 0 us -> 12.1 us
    reduce_scatter x4 -> x0, waiting for transfers between devices: 258 us -> none  [the longest x1 68.7 us: per_device(): lax.psum_scatter(resp_dv.astype(jnp.bfloat16), 'resp', scatter_dimension=...]
    dot_general x104 -> x0, matrix products: 112 us -> none  [the longest x39 38.9 us: block_scores(): jnp.einsum('rd,kd->rk', q_flat, key_rows, preferred_element_type=jnp.floa...]
    all_gather x2 -> x0, blocking collectives: 70.2 us -> none  [the longest x1 38.3 us: per_device(): lax.all_gather(k_prefix[0], 'resp', axis=0, tiled=True)]
    ppermute x0 -> x10, waiting for transfers between devices: none -> 39.6 us  [the longest x4 21.1 us: per_device(): lax.ppermute(count, 'prompt', [(i, i ^ step) for i in range(16)])]
    psum x1 -> x0, blocking collectives: 29.1 us -> none  [per_device(): total = lax.psum(count_local, 'prompt')]
    all_to_all x0 -> x3, waiting for transfers between devices: none -> 25.9 us  [spread(): return lax.all_to_all(value, 'resp', 0, 0, axis_index_groups=columns)]
    all_gather x2 -> x0, waiting for transfers between devices: 25.3 us -> none  [the longest x1 25.3 us: per_device(): lax.all_gather(v_resp[0], 'resp', axis=1, tiled=True)]
    ppermute x0 -> x10, starting transfers between devices: none -> 19 us  [the longest x6 14.3 us: swap(): return lax.ppermute(value, 'resp', pair)]
  transfers between devices with their start and end apart: 6 -> 13, of which waited for: 5 -> 9; matrix products, arithmetic and copies ran while one was open for 5% -> 5% of each run, Pallas kernels for 0% -> 2%
where the time goes in v1:
time: 148 us; the launch traced here: 147 us
  waiting for transfers between devices  65.5 us (44%)
  starting transfers between devices  34.7 us (23%)
  blocking collectives  15.2 us (10%)
  Pallas kernels  12.1 us (8%)
  local copies, waits for them, and re-layouts  10.7 us (7%)
  other arithmetic  6.33 us (4%)
  between operations  2.2 us (1%)
    all_to_all x3, waiting for transfers between devices, spread(): return lax.all_to_all(value, 'resp', 0, 0, axis_index_groups=columns)  25.9 us
    ppermute x4, waiting for transfers between devices, per_device(): lax.ppermute(count, 'prompt', [(i, i ^ step) for i in range(16)])  21.1 us
    ppermute x6, waiting for transfers between devices, swap(): return lax.ppermute(value, 'resp', pair)  18.5 us
    all_to_all x3, starting transfers between devices, spread(): return lax.all_to_all(value, 'resp', 0, 0, axis_index_groups=columns)  15.7 us
    all_to_all x1, blocking collectives, spread(): return lax.all_to_all(value, 'resp', 0, 0, axis_index_groups=columns)  15.2 us
    ppermute x6, starting transfers between devices, swap(): return lax.ppermute(value, 'resp', pair)  14.3 us
    unnamed x28, local copies, waits for them, and re-layouts  5.42 us
    pallas_call x1, Pallas kernels, per_device(): call(final_kernel, 10, [shape((1, ROWS, HEADS * HD), BF16), shape((2, ROW...  4.75 us
  transfers between devices with their start and end apart: 13, of which 9 were waited for; matrix products, arithmetic and copies ran while one was open for 5% of the time, Pallas kernels for 2%

profile of v1, /device:TPU:16, one launch (start us, length us, event | category | flops | bytes accessed | tf_op | source)
XLA Modules:
  0.0 146.7 jit_solution(3972434967507129995)
XLA Ops:
  0.6 0.7 pad_maximum_fusion.3
  1.4 0.8 broadcast_in_dim.7
  2.1 8.5 %all-to-all-start = ((bf16[8,2,64,128]{3,2,1,0:T(8,128)(2,1)}), bf16[8,2,64,128]{3,2,1,0:T(8,128)(2,1)S(1)}, u32[]{:S(2)}, u32[]{:S(2)}) async-start(bf16[8,2,64,128]{3,2,1,0:T(8,128)(2,1)} %broadcast_in_dim.7), calls=%async_computation | async-start | bytes 524288 | tf_op jit(solution)/shard_map/all_to_all | solution.py:287
  10.6 0.8 constant_dynamic-slice_fusion.2
  11.4 1.6 %collective-permute-start.6 = (bf16[2,2,64,128]{3,2,1,0:T(8,128)(2,1)S(1)}, bf16[2,2,64,128]{3,2,1,0:T(8,128)(2,1)S(1)}, u32[]{:S(2)}, u32[]{:S(2)}) collective-permute-start(bf16[2,2,64,128]{3,2,1,0:T(8,128)(2,1)S(1)} %pad_maximum_fusion.2), channel_id=1, source_target_pairs={{0,8},{1,9},{2,10},{3,11},{4,12},{5,13},{6,14},{7,15},{8,0},{9,1},... | collective-permute-start | bytes 196616 | tf_op jit(solution)/shard_map/ppermute | solution.py:284
  13.0 2.8 %collective-permute-done.6 = bf16[2,2,64,128]{3,2,1,0:T(8,128)(2,1)S(1)} collective-permute-done((bf16[2,2,64,128]{3,2,1,0:T(8,128)(2,1)S(1)}, bf16[2,2,64,128]{3,2,1,0:T(8,128)(2,1)S(1)}, u32[]{:S(2)}, u32[]{:S(2)}) %collective-permute-start.6) | collective-permute-done | bytes 65568 | tf_op jit(solution)/shard_map/ppermute | solution.py:284
  15.8 6.7 %all-to-all-done.kv_own = bf16[8,2,64,128]{3,2,1,0:T(8,128)(2,1)S(1)} async-done(((bf16[8,2,64,128]{3,2,1,0:T(8,128)(2,1)}), bf16[8,2,64,128]{3,2,1,0:T(8,128)(2,1)S(1)}, u32[]{:S(2)}, u32[]{:S(2)}) %all-to-all-start) | async-done | bytes 262176 | tf_op jit(solution)/shard_map/all_to_all | solution.py:287
  22.5 1.2 broadcast_in_dim.8
  23.7 3.7 %all-to-all-start.1 = ((bf16[8,2,2,2,64,128]{5,4,3,2,1,0:T(8,128)(2,1)}), bf16[8,2,2,2,64,128]{5,4,3,2,1,0:T(8,128)(2,1)S(1)}, u32[]{:S(2)}, u32[]{:S(2)}) async-start(bf16[8,2,2,2,64,128]{5,4,3,2,1,0:T(8,128)(2,1)} %broadcast_in_dim.8), calls=%async_computation.1 | async-start | bytes 2097152 | tf_op jit(solution)/shard_map/all_to_all | solution.py:287
  27.4 0.0 copy-done.13
  27.4 0.6 convert_reduce_fusion.2
  28.0 0.6 broadcast_in_dim.6
  28.6 0.1 collective-permute-start
  28.8 0.0 copy-done
  28.8 0.0 copy-start.2
  28.8 0.0 copy-start.3
  28.8 0.8 pad_maximum_fusion
  29.7 1.5 %collective-permute-start.4 = (bf16[2,2,64,1024]{3,2,1,0:T(8,128)(2,1)}, bf16[2,2,64,1024]{3,2,1,0:T(8,128)(2,1)S(1)}, u32[]{:S(2)}, u32[]{:S(2)}) collective-permute-start(bf16[2,2,64,1024]{3,2,1,0:T(8,128)(2,1)} %pad_maximum_fusion), channel_id=1, source_target_pairs={{0,8},{1,9},{2,10},{3,11},{4,12},{5,13},{6,14},{7,15},{8,0},{9,1},... | collective-permute-start | bytes 1572872 | tf_op jit(solution)/shard_map/ppermute | solution.py:284
  31.2 0.0 collective-permute-done
  31.2 0.7 broadcast_add_fusion
  31.8 2.8 %collective-permute-start.1 = (f32[8,128]{0,1:T(8,128)S(1)}, f32[8,128]{0,1:T(8,128)S(1)}, u32[]{:S(2)}, u32[]{:S(2)}) collective-permute-start(f32[8,128]{0,1:T(8,128)S(1)} %broadcast_add_fusion), channel_id=1, source_target_pairs={{0,32},{16,48},{32,0},{48,16},{64,96},{80,112},{96,64},{112,80},{1... | collective-permute-start | bytes 12296 | tf_op jit(solution)/shard_map/ppermute | solution.py:308
  34.7 0.2 collective-permute-start.5
  34.9 13.3 %collective-permute-done.1 = f32[8,128]{0,1:T(8,128)S(1)} collective-permute-done((f32[8,128]{0,1:T(8,128)S(1)}, f32[8,128]{0,1:T(8,128)S(1)}, u32[]{:S(2)}, u32[]{:S(2)}) %collective-permute-start.1) | collective-permute-done | bytes 4128 | tf_op jit(solution)/shard_map/ppermute | solution.py:308
  48.2 0.7 fusion.4
  48.9 1.4 collective-permute-start.2
  50.3 0.1 fusion.1
  50.3 2.9 %collective-permute-done.2 = f32[8,128]{0,1:T(8,128)S(1)} collective-permute-done((f32[8,128]{0,1:T(8,128)S(1)}, f32[8,128]{0,1:T(8,128)S(1)}, u32[]{:S(2)}, u32[]{:S(2)}) %collective-permute-start.2) | collective-permute-done | bytes 4128 | tf_op jit(solution)/shard_map/ppermute | solution.py:308
  53.3 0.4 collective-permute-start.3
  53.7 0.1 pad_add_fusion.info
  53.8 0.5 slice.33
  54.3 4.8 %collective-permute-done.3 = f32[8,128]{0,1:T(8,128)S(1)} collective-permute-done((f32[8,128]{0,1:T(8,128)S(1)}, f32[8,128]{0,1:T(8,128)S(1)}, u32[]{:S(2)}, u32[]{:S(2)}) %collective-permute-start.3) | collective-permute-done | bytes 4128 | tf_op jit(solution)/shard_map/ppermute | solution.py:308
  59.1 0.5 slice.34
  61.0 0.0 collective-permute-done.4.got
  61.0 0.0 collective-permute-done.5.kv_pair
  61.0 3.6 %shard_map.136 = (bf16[4,512,128]{2,1,0:T(8,128)(2,1)S(1)}, bf16[4,512,128]{2,1,0:T(8,128)(2,1)S(1)}, f32[4,8,512]{2,1,0:T(8,128)S(1)}, f32[64,1024]{1,0:T(8,128)S(1)}, f32[2,8,2,64,128]{4,3,2,1,0:T(8,128)S(1)}) custom-call(s32[4]{0:T(128)S(1)} %pad_add_fusion.info, bf16[1,4,64,1024]{3,2,1,0:T(8,128)(2,1)S(1)} %copy-done, ...), custom_call_target="tpu_custom_call" | custom-call | flops 3221225472 | bytes 4194304 | tf_op jit(solution)/shard_map/pallas_call | solution.py:313
  64.6 1.0 copy-done.4
  65.6 0.8 copy-done.6
  66.4 0.8 copy-done.9
  67.2 0.7 copy-done.11
  67.9 0.0 all-to-all-done.1.kv
  67.9 1.0 copy-done.7
  69.0 1.0 copy-done.10
  70.0 3.8 %shard_map.137 = (f32[4,8,512]{2,1,0:T(8,128)S(1)}, f32[4,512,128]{2,1,0:T(8,128)S(1)}, bf16[8,2,2,2,64,128]{5,4,3,2,1,0:T(8,128)(2,1)}) custom-call(s32[4]{0:T(128)S(1)} %pad_add_fusion.info, bf16[4,512,128]{2,1,0:T(8,128)(2,1)S(1)} %copy-done.7, bf16[4,512,128]{2,1,0:T(8,128)(2,1)S(1)} %copy-done.10, f32[4,8,512]{2,1,0:T(8,128)S(1)} %get-tuple-element.21.stats_in, ...), custom_call_target="tpu_custom_call" | custom-call | flops 3221225472 | bytes 4194304 | tf_op jit(solution)/shard_map/pallas_call | solution.py:321
  73.8 0.0 copy-done.5
  73.8 0.0 copy-done.12
  73.8 4.7 %shard_map.138 = (bf16[1,64,1024]{2,1,0:T(8,128)(2,1)}, bf16[2,64,1024]{2,1,0:T(8,128)(2,1)S(1)}, bf16[2,64,1024]{2,1,0:T(8,128)(2,1)S(1)}, f32[8,2,64,128]{3,2,1,0:T(8,128)S(1)}, bf16[8,2,64,128]{3,2,1,0:T(8,128)(2,1)S(1)}) custom-call(s32[4]{0:T(128)S(1)} %pad_add_fusion.info, f32[1]{0:T(128)} %bitcast.3.token_scale, bf16[4,512,128]{2,1,0:T(8,128)(2,1)S(1)} %copy-done.8, ...), custom_call_target="tpu_custom_call" | custom-call | flops 4294967296 | bytes 4194304 | tf_op jit(solution)/shard_map/pallas_call | solution.py:329
  78.6 7.5 %collective-permute-start.8 = (bf16[8,2,64,128]{3,2,1,0:T(8,128)(2,1)S(1)}, bf16[8,2,64,128]{3,2,1,0:T(8,128)(2,1)S(1)}, u32[]{:S(2)}, u32[]{:S(2)}) collective-permute-start(bf16[8,2,64,128]{3,2,1,0:T(8,128)(2,1)S(1)} %get-tuple-element.30), channel_id=1, source_target_pairs={{0,8},{1,9},{2,10},{3,11},{4,12},{5,13},{6,14},{7,15},{8,0},{9,1},... | collective-permute-start | bytes 786440 | tf_op jit(solution)/shard_map/ppermute | solution.py:284
  86.1 6.5 %collective-permute-done.8 = bf16[8,2,64,128]{3,2,1,0:T(8,128)(2,1)S(1)} collective-permute-done((bf16[8,2,64,128]{3,2,1,0:T(8,128)(2,1)S(1)}, bf16[8,2,64,128]{3,2,1,0:T(8,128)(2,1)S(1)}, u32[]{:S(2)}, u32[]{:S(2)}) %collective-permute-start.8) | collective-permute-done | bytes 262176 | tf_op jit(solution)/shard_map/ppermute | solution.py:284
  92.7 0.1 add_convert_fusion
  92.8 15.2 %all_to_all.20 = bf16[8,2,64,128]{3,2,1,0:T(8,128)(2,1)S(1)} all-to-all(bf16[8,2,64,128]{3,2,1,0:T(8,128)(2,1)S(1)} %add_convert_fusion), channel_id=1, replica_groups={{0,1,2,3,4,5,6,7},{8,9,10,11,12,13,14,15},{16,17,18,19,20,21,22,23},{24..., dimensions={0} | all-to-all | bytes 524288 | tf_op jit(solution)/shard_map/all_to_all | solution.py:287
  107.9 3.6 %all-to-all-start.3 = ((bf16[8,2,2,2,64,128]{5,4,3,2,1,0:T(8,128)(2,1)}), bf16[8,2,2,2,64,128]{5,4,3,2,1,0:T(8,128)(2,1)S(1)}, u32[]{:S(2)}, u32[]{:S(2)}) async-start(bf16[8,2,2,2,64,128]{5,4,3,2,1,0:T(8,128)(2,1)} %get-tuple-element.31), calls=%async_computation.3 | async-start | bytes 2097152 | tf_op jit(solution)/shard_map/all_to_all | solution.py:287
  111.5 2.1 %collective-permute-start.7 = (bf16[2,64,1024]{2,1,0:T(8,128)(2,1)S(1)}, bf16[2,64,1024]{2,1,0:T(8,128)(2,1)S(1)}, u32[]{:S(2)}, u32[]{:S(2)}) collective-permute-start(bf16[2,64,1024]{2,1,0:T(8,128)(2,1)S(1)} %get-tuple-element.28), channel_id=1, source_target_pairs={{0,8},{1,9},{2,10},{3,11},{4,12},{5,13},{6,14},{7,15},{8,0},{9,1},... | collective-permute-start | bytes 786440 | tf_op jit(solution)/shard_map/ppermute | solution.py:284
  113.6 0.1 maximum_bitcast_fusion.1
  113.7 6.2 %collective-permute-done.7 = bf16[2,64,1024]{2,1,0:T(8,128)(2,1)S(1)} collective-permute-done((bf16[2,64,1024]{2,1,0:T(8,128)(2,1)S(1)}, bf16[2,64,1024]{2,1,0:T(8,128)(2,1)S(1)}, u32[]{:S(2)}, u32[]{:S(2)}) %collective-permute-start.7) | collective-permute-done | bytes 262176 | tf_op jit(solution)/shard_map/ppermute | solution.py:284
  119.9 0.9 maximum_select_fusion
  120.8 0.1 broadcast_multiply_fusion.1
  120.8 0.6 fusion.3
  121.5 19.3 %all-to-all-done.3 = bf16[8,2,2,2,64,128]{5,4,3,2,1,0:T(8,128)(2,1)S(1)} async-done(((bf16[8,2,2,2,64,128]{5,4,3,2,1,0:T(8,128)(2,1)}), bf16[8,2,2,2,64,128]{5,4,3,2,1,0:T(8,128)(2,1)S(1)}, u32[]{:S(2)}, u32[]{:S(2)}) %all-to-all-start.3) | async-done | bytes 1048608 | tf_op jit(solution)/shard_map/all_to_all | solution.py:287
  140.7 0.2 convert_reduce_fusion
  140.9 0.1 broadcast_multiply_fusion
  141.0 1.4 collective-permute-start.9
  142.4 2.9 %collective-permute-done.9 = bf16[2,2,64,128]{3,2,1,0:T(8,128)(2,1)S(1)} collective-permute-done((bf16[2,2,64,128]{3,2,1,0:T(8,128)(2,1)S(1)}, bf16[2,2,64,128]{3,2,1,0:T(8,128)(2,1)S(1)}, u32[]{:S(2)}, u32[]{:S(2)}) %collective-permute-start.9) | collective-permute-done | bytes 65568 | tf_op jit(solution)/shard_map/ppermute | solution.py:284
  145.4 0.7 maximum_select_fusion.2
  146.1 0.7 maximum_select_fusion.1
  (25 shorter events, 0.2 us)
Async XLA Ops:
  2.1 20.3 %all-to-all-start = ((bf16[8,2,64,128]{3,2,1,0:T(8,128)(2,1)}), bf16[8,2,64,128]{3,2,1,0:T(8,128)(2,1)S(1)}, u32[]{:S(2)}, u32[]{:S(2)}) async-start(bf16[8,2,64,128]{3,2,1,0:T(8,128)(2,1)} %broadcast_in_dim.7), calls=%async_computation | async-start | bytes 524288 | tf_op jit(solution)/shard_map/all_to_all | solution.py:287
  11.4 4.4 %collective-permute-start.6 = (bf16[2,2,64,128]{3,2,1,0:T(8,128)(2,1)S(1)}, bf16[2,2,64,128]{3,2,1,0:T(8,128)(2,1)S(1)}, u32[]{:S(2)}, u32[]{:S(2)}) collective-permute-start(bf16[2,2,64,128]{3,2,1,0:T(8,128)(2,1)S(1)} %pad_maximum_fusion.2), channel_id=1, source_target_pairs={{0,8},{1,9},{2,10},{3,11},{4,12},{5,13},{6,14},{7,15},{8,0},{9,1},... | collective-permute-start | bytes 196616 | tf_op jit(solution)/shard_map/ppermute | solution.py:284
  23.7 3.7 %copy-start.13 = (s32[1,4]{1,0:T(1,128)S(1)}, s32[1,4]{1,0:T(1,128)}, u32[]{:S(2)}) copy-start(s32[1,4]{1,0:T(1,128)} %param.17) | copy-start | bytes 52
  23.7 5.1 %copy-start = (bf16[1,4,64,1024]{3,2,1,0:T(8,128)(2,1)S(1)}, bf16[1,4,64,1024]{3,2,1,0:T(8,128)(2,1)}, u32[]{:S(2)}) copy-start(bf16[1,4,64,1024]{3,2,1,0:T(8,128)(2,1)} %qr.1) | copy-start | bytes 1572868
  23.7 5.1 %copy-start.1 = (bf16[1,4,64,1024]{3,2,1,0:T(8,128)(2,1)S(1)}, bf16[1,4,64,1024]{3,2,1,0:T(8,128)(2,1)}, u32[]{:S(2)}) copy-start(bf16[1,4,64,1024]{3,2,1,0:T(8,128)(2,1)} %dr.1) | copy-start | bytes 1572868
  23.7 44.2 %all-to-all-start.1 = ((bf16[8,2,2,2,64,128]{5,4,3,2,1,0:T(8,128)(2,1)}), bf16[8,2,2,2,64,128]{5,4,3,2,1,0:T(8,128)(2,1)S(1)}, u32[]{:S(2)}, u32[]{:S(2)}) async-start(bf16[8,2,2,2,64,128]{5,4,3,2,1,0:T(8,128)(2,1)} %broadcast_in_dim.8), calls=%async_computation.1 | async-start | bytes 2097152 | tf_op jit(solution)/shard_map/all_to_all | solution.py:287
  28.6 2.5 %collective-permute-start = (f32[8,128]{0,1:T(8,128)S(1)}, f32[8,128]{0,1:T(8,128)S(1)}, u32[]{:S(2)}, u32[]{:S(2)}) collective-permute-start(f32[8,128]{0,1:T(8,128)S(1)} %broadcast_in_dim.6), channel_id=1, source_target_pairs={{0,16},{16,0},{32,48},{48,32},{64,80},{80,64},{96,112},{112,96},{1... | collective-permute-start | bytes 12296 | tf_op jit(solution)/shard_map/ppermute | solution.py:308
  28.8 32.2 %copy-start.2 = (bf16[1,64,1024]{2,1,0:T(8,128)(2,1)S(1)}, bf16[1,64,1024]{2,1,0:T(8,128)(2,1)}, u32[]{:S(2)}) copy-start(bf16[1,64,1024]{2,1,0:T(8,128)(2,1)} %qp.1) | copy-start | bytes 393220
  28.8 32.2 %copy-start.3 = (bf16[1,64,1024]{2,1,0:T(8,128)(2,1)S(1)}, bf16[1,64,1024]{2,1,0:T(8,128)(2,1)}, u32[]{:S(2)}) copy-start(bf16[1,64,1024]{2,1,0:T(8,128)(2,1)} %dp.1) | copy-start | bytes 393220
  29.7 31.3 %collective-permute-start.4 = (bf16[2,2,64,1024]{3,2,1,0:T(8,128)(2,1)}, bf16[2,2,64,1024]{3,2,1,0:T(8,128)(2,1)S(1)}, u32[]{:S(2)}, u32[]{:S(2)}) collective-permute-start(bf16[2,2,64,1024]{3,2,1,0:T(8,128)(2,1)} %pad_maximum_fusion), channel_id=1, source_target_pairs={{0,8},{1,9},{2,10},{3,11},{4,12},{5,13},{6,14},{7,15},{8,0},{9,1},... | collective-permute-start | bytes 1572872 | tf_op jit(solution)/shard_map/ppermute | solution.py:284
  31.8 16.4 %collective-permute-start.1 = (f32[8,128]{0,1:T(8,128)S(1)}, f32[8,128]{0,1:T(8,128)S(1)}, u32[]{:S(2)}, u32[]{:S(2)}) collective-permute-start(f32[8,128]{0,1:T(8,128)S(1)} %broadcast_add_fusion), channel_id=1, source_target_pairs={{0,32},{16,48},{32,0},{48,16},{64,96},{80,112},{96,64},{112,80},{1... | collective-permute-start | bytes 12296 | tf_op jit(solution)/shard_map/ppermute | solution.py:308
  34.7 26.3 %collective-permute-start.5 = (bf16[8,2,64,128]{3,2,1,0:T(8,128)(2,1)S(1)}, bf16[8,2,64,128]{3,2,1,0:T(8,128)(2,1)S(1)}, u32[]{:S(2)}, u32[]{:S(2)}) collective-permute-start(bf16[8,2,64,128]{3,2,1,0:T(8,128)(2,1)S(1)} %all-to-all-done.kv_own), channel_id=1, source_target_pairs={{0,8},{1,9},{2,10},{3,11},{4,12},{5,13},{6,14},{7,15},{8,0},{9,1},... | collective-permute-start | bytes 786440 | tf_op jit(solution)/shard_map/ppermute | solution.py:284
  48.9 4.4 %collective-permute-start.2 = (f32[8,128]{0,1:T(8,128)S(1)}, f32[8,128]{0,1:T(8,128)S(1)}, u32[]{:S(2)}, u32[]{:S(2)}) collective-permute-start(f32[8,128]{0,1:T(8,128)S(1)} %fusion.4), channel_id=1, source_target_pairs={{0,64},{16,80},{32,96},{48,112},{64,0},{80,16},{96,32},{112,48},{1... | collective-permute-start | bytes 12296 | tf_op jit(solution)/shard_map/ppermute | solution.py:308
  53.3 5.9 %collective-permute-start.3 = (f32[8,128]{0,1:T(8,128)S(1)}, f32[8,128]{0,1:T(8,128)S(1)}, u32[]{:S(2)}, u32[]{:S(2)}) collective-permute-start(f32[8,128]{0,1:T(8,128)S(1)} %add.35), channel_id=1, source_target_pairs={{0,128},{16,144},{32,160},{48,176},{64,192},{80,208},{96,224},{112... | collective-permute-start | bytes 12296 | tf_op jit(solution)/shard_map/ppermute | solution.py:308
  64.6 1.0 copy-start.4
  65.6 0.8 copy-start.6
  66.4 0.8 copy-start.9
  67.2 0.7 copy-start.11
  67.9 1.0 copy-start.7
  69.0 1.0 copy-start.10
  70.0 3.8 %copy-start.5 = (f32[2,8,2,64,128]{4,3,2,1,0:T(8,128)S(1)}, f32[2,8,2,64,128]{4,3,2,1,0:T(8,128)}, u32[]{:S(2)}) copy-start(f32[2,8,2,64,128]{4,3,2,1,0:T(8,128)} %copy-done.4) | copy-start | bytes 3145732
  70.0 3.8 %copy-start.8 = (bf16[4,512,128]{2,1,0:T(8,128)(2,1)S(1)}, bf16[4,512,128]{2,1,0:T(8,128)(2,1)}, u32[]{:S(2)}) copy-start(bf16[4,512,128]{2,1,0:T(8,128)(2,1)} %copy-done.6) | copy-start | bytes 1572868
  70.0 3.8 %copy-start.12 = (f32[64,1024]{1,0:T(8,128)S(1)}, f32[64,1024]{1,0:T(8,128)}, u32[]{:S(2)}) copy-start(f32[64,1024]{1,0:T(8,128)} %copy-done.11) | copy-start | bytes 786436
  78.6 14.1 %collective-permute-start.8 = (bf16[8,2,64,128]{3,2,1,0:T(8,128)(2,1)S(1)}, bf16[8,2,64,128]{3,2,1,0:T(8,128)(2,1)S(1)}, u32[]{:S(2)}, u32[]{:S(2)}) collective-permute-start(bf16[8,2,64,128]{3,2,1,0:T(8,128)(2,1)S(1)} %get-tuple-element.30), channel_id=1, source_target_pairs={{0,8},{1,9},{2,10},{3,11},{4,12},{5,13},{6,14},{7,15},{8,0},{9,1},... | collective-permute-start | bytes 786440 | tf_op jit(solution)/shard_map/ppermute | solution.py:284
  107.9 32.8 %all-to-all-start.3 = ((bf16[8,2,2,2,64,128]{5,4,3,2,1,0:T(8,128)(2,1)}), bf16[8,2,2,2,64,128]{5,4,3,2,1,0:T(8,128)(2,1)S(1)}, u32[]{:S(2)}, u32[]{:S(2)}) async-start(bf16[8,2,2,2,64,128]{5,4,3,2,1,0:T(8,128)(2,1)} %get-tuple-element.31), calls=%async_computation.3 | async-start | bytes 2097152 | tf_op jit(solution)/shard_map/all_to_all | solution.py:287
  111.5 8.4 %collective-permute-start.7 = (bf16[2,64,1024]{2,1,0:T(8,128)(2,1)S(1)}, bf16[2,64,1024]{2,1,0:T(8,128)(2,1)S(1)}, u32[]{:S(2)}, u32[]{:S(2)}) collective-permute-start(bf16[2,64,1024]{2,1,0:T(8,128)(2,1)S(1)} %get-tuple-element.28), channel_id=1, source_target_pairs={{0,8},{1,9},{2,10},{3,11},{4,12},{5,13},{6,14},{7,15},{8,0},{9,1},... | collective-permute-start | bytes 786440 | tf_op jit(solution)/shard_map/ppermute | solution.py:284
  141.0 4.4 %collective-permute-start.9 = (bf16[2,2,64,128]{3,2,1,0:T(8,128)(2,1)S(1)}, bf16[2,2,64,128]{3,2,1,0:T(8,128)(2,1)S(1)}, u32[]{:S(2)}, u32[]{:S(2)}) collective-permute-start(bf16[2,2,64,128]{3,2,1,0:T(8,128)(2,1)S(1)} %fusion), channel_id=1, source_target_pairs={{0,8},{1,9},{2,10},{3,11},{4,12},{5,13},{6,14},{7,15},{8,0},{9,1},... | collective-permute-start | bytes 196616 | tf_op jit(solution)/shard_map/ppermute | solution.py:284
